TPU v7x, 512 devices: a whole 4x8x8 slice. The times are simulated.
512 devices in a mesh: dp: 2 (over core), ctx: 64 (over z, y), tensor: 4 (over x).
Axes of the slice: x: 4, y: 8, z: 8, core: 2. Of those that a mesh axis runs over, the one named last changes fastest.
Arguments:
- queries: bfloat16 [2, 8192, 4096], P('dp', 'ctx', 'tensor'), may hold values from -6 to 6
- keys: bfloat16 [2, 8192, 4096], P('dp', 'ctx', 'tensor'), may hold values from -6 to 6
- values: bfloat16 [2, 8192, 4096], P('dp', 'ctx', 'tensor'), may hold values from -6 to 6
- forget: float32 [2, 32, 8192], P('dp', 'tensor', 'ctx'), may hold values from 0 to 2
- gain: float32 [4096], P('tensor'), may hold values from 0.1 to 1.9
- grad_out: bfloat16 [2, 8192, 4096], P('dp', 'ctx', 'tensor'), may hold values from -8 to 8
Outputs:
- grad_queries: bfloat16 [2, 8192, 4096], P('dp', 'ctx', 'tensor')
- grad_keys: bfloat16 [2, 8192, 4096], P('dp', 'ctx', 'tensor')
- grad_values: bfloat16 [2, 8192, 4096], P('dp', 'ctx', 'tensor')
- grad_gain: float32 [4096], P('tensor')
All inputs are finite; a program needn't handle non-finite values.
Results may differ from a plain program's by a relative error of at most 0.0062.
Values sent between devices are 32-bit elements; how exact they have to be, the bound alone decides.
A program may use at most 128 MiB of HBM per device.

v0:
```python
import jax
import jax.numpy as jnp
from jax import lax
from jax.sharding import PartitionSpec as P

E = 128


EPSILON = 1e-05


def prefix(value, axis, combine, identity, reverse):
    peers, mine = (lax.axis_size(axis), lax.axis_index(axis))
    everything = jax.tree.map(lambda part: lax.all_gather(part, axis), value)
    start = jax.tree.map(
        lambda part, zero: jnp.broadcast_to(jnp.asarray(zero, part.dtype), part.shape),
        value,
        identity,
    )

    def step(k, before):
        at = peers - 1 - k if reverse else k
        reached = at > mine if reverse else at < mine
        new = combine(before, jax.tree.map(lambda part: part[at], everything))
        return jax.tree.map(lambda a, b: jnp.where(reached, a, b), new, before)

    return lax.fori_loop(0, peers, step, start)


def decay_parts(forget_now):
    cumulative = jnp.cumsum(forget_now, axis=1)
    spans_all = cumulative[:, :, None] - cumulative[:, None, :]
    positions = jnp.arange(forget_now.shape[1])
    lower_mask = (positions[:, None] >= positions[None, :])[None]
    weight = jnp.where(lower_mask, jnp.exp(-jnp.where(lower_mask, spans_all, 0.0)), 0.0)
    return (cumulative, weight)


def merge_states(earlier, later):
    return (earlier[0] + later[0], jnp.exp(-later[0])[:, None, None] * earlier[1] + later[1])


def gain_total(partial_gain):
    return lax.psum(partial_gain, ("dp", "ctx"))


def shards(queries, keys, values, forget, gain, grad_out):
    rows = queries.shape[1]
    heads = gain.shape[0] // E
    full_width = lax.axis_size("tensor") * gain.shape[0]
    score_scale = E ** (-0.5)
    query_rows = queries[0].reshape(rows, heads, E)
    key_rows = keys[0].reshape(rows, heads, E)
    value_rows = values[0].reshape(rows, heads, E)
    grad_rows = grad_out[0].reshape(rows, heads, E).astype(jnp.float32)
    cumulative, weight = decay_parts(forget[0])
    block_decay = cumulative[:, -1]
    query_decay = jnp.exp(-cumulative).T[:, :, None]
    key_decay = jnp.exp(-(block_decay[:, None] - cumulative)).T[:, :, None]
    weighted = (
        jnp.einsum("the,she->hts", query_rows, key_rows, preferred_element_type=jnp.float32)
        * score_scale
        * weight
    ).astype(jnp.bfloat16)
    key_scaled = (key_rows.astype(jnp.float32) * key_decay).astype(jnp.bfloat16)
    own_state = jnp.einsum(
        "she,shf->hef", key_scaled, value_rows, preferred_element_type=jnp.float32
    )
    zero_decay = jnp.zeros_like(block_decay)
    zero_state = jnp.zeros_like(own_state)
    earlier_state = prefix(
        (block_decay, own_state), "ctx", merge_states, (zero_decay, zero_state), False
    )[1]
    earlier_b = earlier_state.astype(jnp.bfloat16)
    attended = jnp.einsum(
        "hts,shf->thf", weighted, value_rows, preferred_element_type=jnp.float32
    ) + score_scale * query_decay * jnp.einsum(
        "the,hef->thf", query_rows, earlier_b, preferred_element_type=jnp.float32
    )
    grad_normed = grad_rows * gain.reshape(heads, E)[None]
    squares = jnp.sum(attended * attended, axis=(1, 2))
    square_all = lax.psum(squares, "tensor")
    inverse_rms = lax.rsqrt(square_all / full_width + EPSILON)
    normed = attended * inverse_rms[:, None, None]
    projected = lax.psum(jnp.sum(grad_normed * normed, axis=(1, 2)), "tensor") / full_width
    grad_attended = (
        inverse_rms[:, None, None] * (grad_normed - normed * projected[:, None, None])
    ).astype(jnp.bfloat16)
    grad_gain = gain_total(jnp.sum(grad_rows * normed, axis=0).reshape(-1))
    query_scaled = (query_rows.astype(jnp.float32) * query_decay).astype(jnp.bfloat16)
    own_back = jnp.einsum(
        "the,thf->hef", query_scaled, grad_attended, preferred_element_type=jnp.float32
    )
    later_state = prefix(
        (block_decay, own_back), "ctx", merge_states, (zero_decay, zero_state), True
    )[1]
    later_b = later_state.astype(jnp.bfloat16)
    grad_weighted = (
        jnp.einsum("thf,shf->hts", grad_attended, value_rows, preferred_element_type=jnp.float32)
        * score_scale
        * weight
    ).astype(jnp.bfloat16)
    grad_q = jnp.einsum(
        "hts,she->the", grad_weighted, key_rows, preferred_element_type=jnp.float32
    ) + score_scale * query_decay * jnp.einsum(
        "thf,hef->the", grad_attended, earlier_b, preferred_element_type=jnp.float32
    )
    grad_k = jnp.einsum(
        "hts,the->she", grad_weighted, query_rows, preferred_element_type=jnp.float32
    ) + score_scale * key_decay * jnp.einsum(
        "shf,hef->she", value_rows, later_b, preferred_element_type=jnp.float32
    )
    grad_v = jnp.einsum(
        "hts,thf->shf", weighted, grad_attended, preferred_element_type=jnp.float32
    ) + score_scale * key_decay * jnp.einsum(
        "she,hef->shf", key_rows, later_b, preferred_element_type=jnp.float32
    )
    return (
        grad_q.astype(jnp.bfloat16).reshape(1, rows, heads * E),
        grad_k.astype(jnp.bfloat16).reshape(1, rows, heads * E),
        grad_v.astype(jnp.bfloat16).reshape(1, rows, heads * E),
        grad_gain,
    )


def solution(mesh):
    in_specs = (
        P("dp", "ctx", "tensor"),
        P("dp", "ctx", "tensor"),
        P("dp", "ctx", "tensor"),
        P("dp", "tensor", "ctx"),
        P("tensor"),
        P("dp", "ctx", "tensor"),
    )
    out_specs = (
        P("dp", "ctx", "tensor"),
        P("dp", "ctx", "tensor"),
        P("dp", "ctx", "tensor"),
        P("tensor"),
    )
    return jax.shard_map(shards, mesh=mesh, in_specs=in_specs, out_specs=out_specs, check_vma=False)
```

profile of v0, /device:TPU:258, one launch (start us, length us, event | category | flops | bytes accessed | tf_op | source)
XLA Modules:
  0.0 707.8 jit_solution(14197729764191864762)
XLA Ops:
  14.0 1.3 dynamic-slice
  16.2 142.5 %all-reduce = f32[512]{0:T(512)S(1)} all-reduce(f32[512]{0:T(512)S(1)} %dynamic-update-slice), channel_id=2, replica_groups=mesh['dp'=2,'ctx'=64,'tensor'=4] {'ctx'}, use_global_device_ids=true, to_apply=%add | all-reduce | flops 512 | bytes 4096
  159.2 76.4 %all-gather.6.cloned.1.call-done = f32[512,128,128]{2,1,0:T(8,128)} async-done(((f32[8,128,128]{2,1,0:T(8,128)}), f32[512,128,128]{2,1,0:T(8,128)}) %all-gather.6.cloned.1.call-update) | async-done | bytes 33554448 | tf_op jit(solution)/shard_map/all_gather | solution.py:14
  235.6 77.9 %while.30 = (s32[]{:T(128)}, f32[8,128,128]{2,1,0:T(8,128)S(1)}, s32[]{:T(128)}, f32[64,8]{1,0:T(8,128)S(1)}, f32[64,8,128,128]{3,2,1,0:T(8,128)}, /*index=5*/s32[]{:T(128)}, s32[]{:T(128)}) while((s32[]{:T(128)}, f32[8,128,128]{2,1,0:T(8,128)S(1)}, s32[]{:T(128)}, f32[64,8]{1,0:T(8,128)S(1)}, f32[64,8,128,128]{3,2,1,0:T(8,128)}, ...), condition=%wide.region_2.3_spmd.clone, body=%wide.region_1.2_spmd.clone.sunk | while | flops 524300 | bytes 1573073 | solution.py:27
  314.2 8.6 %psum.21 = f32[128]{0:T(128)S(1)} all-reduce(f32[128]{0:T(128)S(1)} %get-tuple-element.305), channel_id=1, replica_groups=mesh['dp'=2,'ctx'=64,'tensor'=4] {'tensor'}, use_global_device_ids=true, to_apply=%region_4.5 | all-reduce | flops 128 | bytes 1024 | tf_op jit(solution)/shard_map/psum | solution.py:82
  323.8 10.1 %psum.22 = f32[128]{0:T(128)S(1)} all-reduce(f32[128]{0:T(128)S(1)} %get-tuple-element.281), channel_id=1, replica_groups=mesh['dp'=2,'ctx'=64,'tensor'=4] {'tensor'}, use_global_device_ids=true, to_apply=%region_6.7 | all-reduce | flops 128 | bytes 1024 | tf_op jit(solution)/shard_map/psum | solution.py:85
  337.7 281.8 %psum.23 = f32[1024]{0:T(1024)} all-reduce(f32[1024]{0:T(1024)S(1)} %bitcast.116), channel_id=1, replica_groups=mesh['dp'=2,'ctx'=64,'tensor'=4] {'dp','ctx'}, use_global_device_ids=true, to_apply=%region_10.11 | all-reduce | flops 1024 | bytes 8192 | tf_op jit(solution)/shard_map/psum | solution.py:44
  619.8 78.6 %while.31 = (s32[]{:T(128)}, f32[8,128,128]{2,1,0:T(8,128)S(1)}, s32[]{:T(128)}, f32[64,8]{1,0:T(8,128)S(1)}, f32[64,8,128,128]{3,2,1,0:T(8,128)}, /*index=5*/s32[]{:T(128)}, s32[]{:T(128)}, s32[]{:T(128)}, s32[]{:T(128)}) while((s32[]{:T(128)}, f32[8,128,128]{2,1,0:T(8,128)S(1)}, s32[]{:T(128)}, f32[64,8]{1,0:T(8,128)S(1)}, ...), condition=%wide.region_8.9_spmd.clone, body=%wide.region_7.8_spmd.clone.sunk | while | flops 524304 | bytes 1573135 | solution.py:27
  619.8 1.2 fusion.46
  621.0 1.2 fusion.46
  622.3 1.2 fusion.46
  623.5 1.2 fusion.46
  624.7 1.2 fusion.46
  625.9 1.2 fusion.46
  627.2 1.2 fusion.46
  628.4 1.2 fusion.46
  629.6 1.2 fusion.46
  630.9 1.2 fusion.46
  632.1 1.2 fusion.46
  633.3 1.2 fusion.46
  634.5 1.2 fusion.46
  635.8 1.2 fusion.46
  637.0 1.2 fusion.46
  638.2 1.2 fusion.46
  641.9 1.2 fusion.46
  646.8 1.2 fusion.46
  660.3 1.2 fusion.46
  665.2 1.2 fusion.46
  670.1 1.2 fusion.46
  683.7 1.2 fusion.46
  688.6 1.2 fusion.46
  693.5 1.2 fusion.46
  (271 shorter events, 139.2 us)
Async XLA Ops:
  7.2 228.4 %all-gather.6.cloned.1.call-start = ((), (), s32[]{:S(2)}) async-start(), calls=%async_computation | async-start | bytes 34078720 | tf_op jit(solution)/shard_map/all_gather | solution.py:14
  11.7 608.0 %all-gather.8.cloned.1.call-start = ((), (), s32[]{:S(2)}) async-start(), calls=%async_computation.1 | async-start | bytes 34078720 | tf_op jit(solution)/shard_map/all_gather | solution.py:14
Sparse Core Ops, SparseCore 0:
  11.8 223.7 all-gather.5
  336.1 221.6 all-gather.7
where the time goes:
time: 714 us; the launch traced here: 708 us
  blocking collectives  443 us (62%)
  other arithmetic  155 us (22%)
  waiting for transfers between devices  76.5 us (11%)
  between operations  14.9 us (2%)
  local copies, waits for them, and re-layouts  8.77 us (1%)
    psum x1, blocking collectives, gain_total(): return lax.psum(partial_gain, ('dp', 'ctx'))  282 us
    select_n x128, other arithmetic, step(): return jax.tree.map(lambda a, b: jnp.where(reached, a, b), new, before)  150 us
    unnamed x1, blocking collectives  143 us
    all_gather x2, waiting for transfers between devices, prefix(): everything = jax.tree.map(lambda part: lax.all_gather(part, axis), value)  76.4 us
  transfers between devices with their start and end apart: 2, of which 1 were waited for; matrix products, arithmetic and copies ran while one was open for 1% of the time, Pallas kernels for 0%

commit v1 on v0

v1 whole, which is shorter than its diff:
```python
import functools

import jax
import jax.numpy as jnp
from jax import lax
from jax.experimental import pallas as pl
from jax.experimental.pallas import tpu as pltpu
from jax.sharding import PartitionSpec as P

E = 128
EPSILON = 1e-05
MESH = pl.DeviceIdType.MESH
F32 = jnp.float32
BF16 = jnp.bfloat16

HEADS = 8
CTX = 64
RING = 8
TENSOR = 4
BATCHES = 2
GROUP = HEADS // BATCHES
OWNERS = CTX // GROUP


def matmul(a, b, contract_a, contract_b):
    return lax.dot_general(
        a, b, (((contract_a,), (contract_b,)), ((), ())), preferred_element_type=F32
    )


def kernel(
    q_ref, k_ref, v_ref, f_ref, gain_ref, g_ref,
    gq_ref, gk_ref, gv_ref, gg_ref,
    state, state_in, prefix, prefix_in,
    back, back_in, suffix, suffix_in,
    decay_out, decay_in,
    weight, weighted, attended, earlier_b, grad_att, part_k, part_v,
    norm_out, norm_in,
    gain_y_out, gain_y_in, gain_z_out, gain_z_in, gain_dp_out, gain_dp_in,
    decay_sems, state_send, state_recv, prefix_send, prefix_recv,
    back_send, back_recv, suffix_send, suffix_recv,
    norm_sems, gain_y_sems, gain_z_sems, gain_dp_sems,
):
    dp, me, tn = lax.axis_index("dp"), lax.axis_index("ctx"), lax.axis_index("tensor")
    z, y = me // RING, lax.rem(me, RING)
    scale = E ** (-0.5)
    full_width = TENSOR * HEADS * E

    def ctx_peer(i):
        return lax.rem(z + i // RING, RING) * RING + lax.rem(y + lax.rem(i, RING), RING)

    def tensor_peer(i):
        return lax.rem(tn + i, TENSOR)

    def y_peer(i):
        return z * RING + lax.rem(y + i, RING)

    def z_peer(i):
        return lax.rem(z + i, RING) * RING + y

    barrier = pltpu.get_barrier_semaphore()

    def greet_ctx(i, carry):
        pl.semaphore_signal(
            barrier, inc=1, device_id=(dp, ctx_peer(i), tn), device_id_type=MESH
        )
        return carry

    def greet_tensor(i, carry):
        pl.semaphore_signal(
            barrier, inc=1, device_id=(dp, me, tensor_peer(i)), device_id_type=MESH
        )
        return carry

    lax.fori_loop(1, CTX, greet_ctx, 0)
    lax.fori_loop(1, TENSOR, greet_tensor, 0)
    pl.semaphore_signal(barrier, inc=1, device_id=(1 - dp, me, tn), device_id_type=MESH)

    def remote(src, dst, send_sem, recv_sem, device):
        return pltpu.make_async_remote_copy(
            src_ref=src, dst_ref=dst, send_sem=send_sem, recv_sem=recv_sem,
            device_id=device, device_id_type=MESH,
        )

    def wait_bytes(ref, sem):
        pltpu.make_async_copy(ref, ref, sem).wait()

    def exchange(src, dst, send_sem, recv_sem):
        def go(i, carry):
            peer = ctx_peer(i)
            remote(src.at[peer], dst.at[me], send_sem, recv_sem, (dp, peer, tn)).start()
            return carry

        lax.fori_loop(1, CTX, go, 0)
        dst[me] = src[me]

    lanes = lax.broadcasted_iota(jnp.int32, (HEADS, E), 1)
    cumulative = f_ref[0]
    for shift in (1, 2, 4, 8, 16, 32, 64):
        moved = pltpu.roll(cumulative, shift, 1)
        cumulative = cumulative + jnp.where(lanes >= shift, moved, 0.0)
    block_decay = cumulative[:, E - 1 :]
    passing = jnp.broadcast_to(jnp.exp(-block_decay), (HEADS, E))
    for h in range(HEADS):
        decay_out[h % GROUP, h // GROUP] = passing[h]
    cumulative_t = cumulative.T
    query_decay = jnp.exp(-cumulative).T
    key_decay = jnp.exp(-(block_decay - cumulative)).T

    def columns(h):
        return slice(h * E, (h + 1) * E)

    def pieces(h):
        return h // GROUP, slice((h % GROUP) * OWNERS, (h % GROUP + 1) * OWNERS)

    def put_state(ref, h, value):
        batch, rows = pieces(h)
        ref[batch, rows] = value.reshape(OWNERS, 8, E)

    def get_state(ref, h):
        batch, rows = pieces(h)
        return ref[batch, rows].reshape(E, E)

    for h in range(HEADS):
        key_scaled = (k_ref[0, :, columns(h)].astype(F32) * key_decay[:, h : h + 1]).astype(BF16)
        put_state(state, h, matmul(key_scaled, v_ref[0, :, columns(h)], 0, 0))

    pl.semaphore_wait(barrier, CTX - 1 + TENSOR - 1 + 1)

    def send_decay(i, carry):
        peer = ctx_peer(i)
        remote(
            decay_out.at[peer // OWNERS], decay_in.at[me],
            decay_sems.at[0], decay_sems.at[1], (dp, peer, tn),
        ).start()
        return carry

    lax.fori_loop(1, CTX, send_decay, 0)
    decay_in[me] = decay_out[me // OWNERS]
    for b in range(BATCHES):
        exchange(state.at[b], state_in.at[b], state_send.at[b], state_recv.at[b])

    below = lax.broadcasted_iota(jnp.int32, (E, E), 0) >= lax.broadcasted_iota(
        jnp.int32, (E, E), 1
    )
    for h in range(HEADS):
        span = cumulative_t[:, h : h + 1] - cumulative[h : h + 1, :]
        now = jnp.where(below, jnp.exp(-jnp.where(below, span, 0.0)), 0.0)
        weight[h] = now
        scores = matmul(q_ref[0, :, columns(h)], k_ref[0, :, columns(h)], 1, 1)
        rounded = (scores * scale * now).astype(BF16)
        weighted[h] = rounded
        attended[h] = matmul(rounded, v_ref[0, :, columns(h)], 1, 0)

    others = pl.ds(0, CTX - 1)
    wait_bytes(decay_in.at[others], decay_sems.at[1])

    def run_scan(b, source, result, reverse):
        def step(i, total):
            at = CTX - 1 - i if reverse else i
            result[b, at] = total
            return total * decay_in[at, b : b + 1] + source[b, at]

        lax.fori_loop(0, CTX, step, jnp.zeros((8, E), F32), unroll=8)

    for b in range(BATCHES):
        wait_bytes(state_in.at[b, others], state_recv.at[b])
        run_scan(b, state_in, prefix, False)
        exchange(prefix.at[b], prefix_in.at[b], prefix_send.at[b], prefix_recv.at[b])

    squares = jnp.zeros((E, E), F32)
    products = jnp.zeros((E, E), F32)
    for b in range(BATCHES):
        wait_bytes(prefix_in.at[b, others], prefix_recv.at[b])
        for h in range(b * GROUP, (b + 1) * GROUP):
            state_b = get_state(prefix_in, h).astype(BF16)
            earlier_b[h] = state_b
            carried = matmul(q_ref[0, :, columns(h)], state_b, 1, 0)
            now = attended[h] + scale * query_decay[:, h : h + 1] * carried
            attended[h] = now
            grad_normed = g_ref[0, :, columns(h)].astype(F32) * gain_ref[h : h + 1, :]
            squares = squares + now * now
            products = products + grad_normed * now

    wide = lax.broadcasted_iota(jnp.int32, (E, E), 1)
    both = jnp.where(
        wide == 0,
        jnp.sum(squares, axis=1, keepdims=True),
        jnp.sum(products, axis=1, keepdims=True),
    ).T[0:8]
    norm_out[...] = both

    def send_norm(i, carry):
        remote(
            norm_out, norm_in.at[tn], norm_sems.at[0], norm_sems.at[1], (dp, me, tensor_peer(i))
        ).start()
        return carry

    lax.fori_loop(1, TENSOR, send_norm, 0)
    norm_in[tn] = both
    wait_bytes(norm_in.at[pl.ds(0, TENSOR - 1)], norm_sems.at[1])
    sums = (norm_in[0] + norm_in[1]) + (norm_in[2] + norm_in[3])
    inverse_rms = lax.rsqrt(sums[0:1] / full_width + EPSILON)
    projected = sums[1:2] * inverse_rms / full_width
    of_grad = jnp.broadcast_to(inverse_rms, (E, E)).T
    of_attended = jnp.broadcast_to(inverse_rms * inverse_rms * projected, (E, E)).T

    for b in range(BATCHES):
        for h in range(b * GROUP, (b + 1) * GROUP):
            grad_normed = g_ref[0, :, columns(h)].astype(F32) * gain_ref[h : h + 1, :]
            grad_now = (of_grad * grad_normed - of_attended * attended[h]).astype(BF16)
            grad_att[h] = grad_now
            query_scaled = (
                q_ref[0, :, columns(h)].astype(F32) * query_decay[:, h : h + 1]
            ).astype(BF16)
            put_state(back, h, matmul(query_scaled, grad_now, 0, 0))
        exchange(back.at[b], back_in.at[b], back_send.at[b], back_recv.at[b])

    for h in range(HEADS):
        normed = attended[h] * of_grad
        gain_y_out[h] = jnp.sum(g_ref[0, :, columns(h)].astype(F32) * normed, axis=0)

    def sum_ring(out, into, sems, peer_of, mine):
        def go(i, carry):
            remote(out, into.at[mine], sems.at[0], sems.at[1], (dp, peer_of(i), tn)).start()
            return carry

        lax.fori_loop(1, RING, go, 0)
        into[mine] = out[...]

    def ring_total(into, sems):
        wait_bytes(into.at[pl.ds(0, RING - 1)], sems.at[1])
        total = into[0]
        for i in range(1, RING):
            total = total + into[i]
        return total

    sum_ring(gain_y_out, gain_y_in, gain_y_sems, y_peer, y)

    for h in range(HEADS):
        grad_now = grad_att[h]
        scores = matmul(grad_now, v_ref[0, :, columns(h)], 1, 1)
        grad_weighted = (scores * scale * weight[h]).astype(BF16)
        grad_q = matmul(grad_weighted, k_ref[0, :, columns(h)], 1, 0) + scale * query_decay[
            :, h : h + 1
        ] * matmul(grad_now, earlier_b[h], 1, 1)
        gq_ref[0, :, columns(h)] = grad_q.astype(BF16)
        part_k[h] = matmul(grad_weighted, q_ref[0, :, columns(h)], 0, 0)
        part_v[h] = matmul(weighted[h], grad_now, 0, 0)

    for b in range(BATCHES):
        wait_bytes(back_in.at[b, others], back_recv.at[b])
        run_scan(b, back_in, suffix, True)
        exchange(suffix.at[b], suffix_in.at[b], suffix_send.at[b], suffix_recv.at[b])

    gain_z_out[...] = ring_total(gain_y_in, gain_y_sems)
    sum_ring(gain_z_out, gain_z_in, gain_z_sems, z_peer, z)
    gain_total = ring_total(gain_z_in, gain_z_sems)
    gain_dp_out[...] = gain_total
    other_core = remote(
        gain_dp_out, gain_dp_in, gain_dp_sems.at[0], gain_dp_sems.at[1], (1 - dp, me, tn)
    )
    other_core.start()

    for b in range(BATCHES):
        wait_bytes(suffix_in.at[b, others], suffix_recv.at[b])
        for h in range(b * GROUP, (b + 1) * GROUP):
            later_b = get_state(suffix_in, h).astype(BF16)
            scaling = scale * key_decay[:, h : h + 1]
            grad_k = part_k[h] + scaling * matmul(v_ref[0, :, columns(h)], later_b, 1, 1)
            grad_v = part_v[h] + scaling * matmul(k_ref[0, :, columns(h)], later_b, 1, 0)
            gk_ref[0, :, columns(h)] = grad_k.astype(BF16)
            gv_ref[0, :, columns(h)] = grad_v.astype(BF16)

    other_core.wait()
    gg_ref[...] = gain_total + gain_dp_in[...]

    wait_bytes(decay_in.at[others], decay_sems.at[0])
    for b in range(BATCHES):
        wait_bytes(state.at[b, others], state_send.at[b])
        wait_bytes(prefix.at[b, others], prefix_send.at[b])
        wait_bytes(back.at[b, others], back_send.at[b])
        wait_bytes(suffix.at[b, others], suffix_send.at[b])
    wait_bytes(norm_in.at[pl.ds(0, TENSOR - 1)], norm_sems.at[0])
    wait_bytes(gain_y_in.at[pl.ds(0, RING - 1)], gain_y_sems.at[0])
    wait_bytes(gain_z_in.at[pl.ds(0, RING - 1)], gain_z_sems.at[0])


def shards(queries, keys, values, forget, gain, grad_out):
    block = jax.ShapeDtypeStruct(queries.shape, BF16)
    states = pltpu.VMEM((BATCHES, CTX, 8, E), F32)
    squares_f32 = pltpu.VMEM((HEADS, E, E), F32)
    squares_bf16 = pltpu.VMEM((HEADS, E, E), BF16)
    tile = pltpu.VMEM((8, E), F32)
    ring = pltpu.VMEM((RING, 8, E), F32)
    pair = pltpu.SemaphoreType.DMA((2,))
    vmem = pl.BlockSpec(memory_space=pltpu.VMEM)
    grad_q, grad_k, grad_v, grad_gain = pl.pallas_call(
        kernel,
        out_shape=(block, block, block, jax.ShapeDtypeStruct((HEADS, E), F32)),
        in_specs=[vmem] * 6,
        out_specs=(vmem,) * 4,
        scratch_shapes=[states] * 8
        + [pltpu.VMEM((GROUP, BATCHES, E), F32), pltpu.VMEM((CTX, BATCHES, E), F32)]
        + [squares_f32, squares_bf16, squares_f32, squares_bf16, squares_bf16]
        + [squares_f32, squares_f32]
        + [tile, pltpu.VMEM((TENSOR, 8, E), F32)]
        + [tile, ring, tile, ring, tile, tile]
        + [pair] * 13,
        compiler_params=pltpu.CompilerParams(
            collective_id=0, has_side_effects=True, vmem_limit_bytes=40 << 20
        ),
    )(queries, keys, values, forget, gain.reshape(HEADS, E), grad_out)
    return grad_q, grad_k, grad_v, grad_gain.reshape(-1)


def solution(mesh):
    in_specs = (
        P("dp", "ctx", "tensor"),
        P("dp", "ctx", "tensor"),
        P("dp", "ctx", "tensor"),
        P("dp", "tensor", "ctx"),
        P("tensor"),
        P("dp", "ctx", "tensor"),
    )
    out_specs = (
        P("dp", "ctx", "tensor"),
        P("dp", "ctx", "tensor"),
        P("dp", "ctx", "tensor"),
        P("tensor"),
    )
    return jax.shard_map(shards, mesh=mesh, in_specs=in_specs, out_specs=out_specs, check_vma=False)
```

time: 714 us -> 87.8 us (0.12)
  the two profiles are of different devices: /device:TPU:258 before, /device:TPU:1 now
where the time goes in v1:
time: 87.8 us; the launch traced here: 87.5 us
  Pallas kernels  79 us (90%)
  local copies, waits for them, and re-layouts  7.87 us (9%)
    pallas_call x1, Pallas kernels, shards(): pl.pallas_call(kernel, out_shape=(block, block, block, jax.ShapeDtypeStru...  79 us
    unnamed x16, local copies, waits for them, and re-layouts  7.87 us

profile of v1, /device:TPU:1, one launch (start us, length us, event | category | flops | bytes accessed | tf_op | source)
XLA Modules:
  0.0 87.5 jit_solution(10501641013429572096)
XLA Ops:
  0.6 0.0 copy-start
  0.6 0.9 %copy-done = bf16[1,128,1024]{2,1,0:T(8,128)(2,1)S(1)} copy-done((bf16[1,128,1024]{2,1,0:T(8,128)(2,1)S(1)}, bf16[1,128,1024]{2,1,0:T(8,128)(2,1)}, u32[]{:S(2)}) %copy-start) | copy-done | bytes 262168
  1.6 0.0 copy-start.1
  1.6 0.9 %copy-done.1 = bf16[1,128,1024]{2,1,0:T(8,128)(2,1)S(1)} copy-done((bf16[1,128,1024]{2,1,0:T(8,128)(2,1)S(1)}, bf16[1,128,1024]{2,1,0:T(8,128)(2,1)}, u32[]{:S(2)}) %copy-start.1) | copy-done | bytes 262168
  2.5 0.0 copy-start.2
  2.5 0.9 %copy-done.2 = bf16[1,128,1024]{2,1,0:T(8,128)(2,1)S(1)} copy-done((bf16[1,128,1024]{2,1,0:T(8,128)(2,1)S(1)}, bf16[1,128,1024]{2,1,0:T(8,128)(2,1)}, u32[]{:S(2)}) %copy-start.2) | copy-done | bytes 262168
  3.5 0.0 copy-start.3
  3.5 0.9 %copy-done.3 = bf16[1,128,1024]{2,1,0:T(8,128)(2,1)S(1)} copy-done((bf16[1,128,1024]{2,1,0:T(8,128)(2,1)S(1)}, bf16[1,128,1024]{2,1,0:T(8,128)(2,1)}, u32[]{:S(2)}) %copy-start.3) | copy-done | bytes 262168
  4.4 0.0 copy-start.4
  4.4 0.7 copy-done.4
  5.1 0.0 copy-start.5
  5.1 0.7 copy-done.5
  5.8 79.0 %shard_map.93 = (bf16[1,128,1024]{2,1,0:T(8,128)(2,1)S(1)}, bf16[1,128,1024]{2,1,0:T(8,128)(2,1)S(1)}, bf16[1,128,1024]{2,1,0:T(8,128)(2,1)S(1)}, f32[8,128]{1,0:T(8,128)S(1)}) custom-call(bf16[1,128,1024]{2,1,0:T(8,128)(2,1)S(1)} %copy-done, bf16[1,128,1024]{2,1,0:T(8,128)(2,1)S(1)} %copy-done.1, bf16[1,128,1024]{2,1,0:T(8,128)(2,1)S(1)} %copy-done.2, ...), custom_call_target="tpu_custom_call" | custom-call | tf_op jit(solution)/shard_map/pallas_call | solution.py:298
  84.8 0.7 copy.14
  85.5 0.7 copy.15
  86.2 0.7 copy.16
  86.9 0.6 copy.17
Async XLA Ops:
  0.6 1.0 %copy-start = (bf16[1,128,1024]{2,1,0:T(8,128)(2,1)S(1)}, bf16[1,128,1024]{2,1,0:T(8,128)(2,1)}, u32[]{:S(2)}) copy-start(bf16[1,128,1024]{2,1,0:T(8,128)(2,1)} %q_ref.1) | copy-start | bytes 786436
  1.6 0.9 %copy-start.1 = (bf16[1,128,1024]{2,1,0:T(8,128)(2,1)S(1)}, bf16[1,128,1024]{2,1,0:T(8,128)(2,1)}, u32[]{:S(2)}) copy-start(bf16[1,128,1024]{2,1,0:T(8,128)(2,1)} %k_ref.1) | copy-start | bytes 786436
  2.5 0.9 %copy-start.2 = (bf16[1,128,1024]{2,1,0:T(8,128)(2,1)S(1)}, bf16[1,128,1024]{2,1,0:T(8,128)(2,1)}, u32[]{:S(2)}) copy-start(bf16[1,128,1024]{2,1,0:T(8,128)(2,1)} %v_ref.1) | copy-start | bytes 786436
  3.5 0.9 %copy-start.3 = (bf16[1,128,1024]{2,1,0:T(8,128)(2,1)S(1)}, bf16[1,128,1024]{2,1,0:T(8,128)(2,1)}, u32[]{:S(2)}) copy-start(bf16[1,128,1024]{2,1,0:T(8,128)(2,1)} %g_ref.1) | copy-start | bytes 786436
  4.4 0.7 copy-start.4
  5.1 0.7 copy-start.5

commit v2 on v1

--- a/solution.py
+++ b/solution.py
@@ -29,8 +29,9 @@
 
 
 def kernel(
+    q_hbm, k_hbm, v_hbm, f_hbm, gain_hbm, g_hbm,
+    gq_ref, gk_ref, gv_ref, gg_ref,
     q_ref, k_ref, v_ref, f_ref, gain_ref, g_ref,
-    gq_ref, gk_ref, gv_ref, gg_ref,
     state, state_in, prefix, prefix_in,
     back, back_in, suffix, suffix_in,
     decay_out, decay_in,
@@ -39,7 +40,7 @@
     gain_y_out, gain_y_in, gain_z_out, gain_z_in, gain_dp_out, gain_dp_in,
     decay_sems, state_send, state_recv, prefix_send, prefix_recv,
     back_send, back_recv, suffix_send, suffix_recv,
-    norm_sems, gain_y_sems, gain_z_sems, gain_dp_sems,
+    norm_sems, gain_y_sems, gain_z_sems, gain_dp_sems, load_sems,
 ):
     dp, me, tn = lax.axis_index("dp"), lax.axis_index("ctx"), lax.axis_index("tensor")
     z, y = me // RING, lax.rem(me, RING)
@@ -58,6 +59,18 @@
     def z_peer(i):
         return lax.rem(z + i, RING) * RING + y
 
+    loads = [
+        pltpu.make_async_copy(source, target, load_sems.at[i])
+        for i, (source, target) in enumerate(
+            (
+                (f_hbm, f_ref), (k_hbm, k_ref), (v_hbm, v_ref),
+                (q_hbm, q_ref), (g_hbm, g_ref), (gain_hbm, gain_ref),
+            )
+        )
+    ]
+    for load in loads:
+        load.start()
+
     barrier = pltpu.get_barrier_semaphore()
 
     def greet_ctx(i, carry):
@@ -94,6 +107,7 @@
         lax.fori_loop(1, CTX, go, 0)
         dst[me] = src[me]
 
+    loads[0].wait()
     lanes = lax.broadcasted_iota(jnp.int32, (HEADS, E), 1)
     cumulative = f_ref[0]
     for shift in (1, 2, 4, 8, 16, 32, 64):
@@ -121,6 +135,8 @@
         batch, rows = pieces(h)
         return ref[batch, rows].reshape(E, E)
 
+    loads[1].wait()
+    loads[2].wait()
     for h in range(HEADS):
         key_scaled = (k_ref[0, :, columns(h)].astype(F32) * key_decay[:, h : h + 1]).astype(BF16)
         put_state(state, h, matmul(key_scaled, v_ref[0, :, columns(h)], 0, 0))
@@ -135,10 +151,13 @@
         ).start()
         return carry
 
+    exchange(state.at[0], state_in.at[0], state_send.at[0], state_recv.at[0])
     lax.fori_loop(1, CTX, send_decay, 0)
     decay_in[me] = decay_out[me // OWNERS]
-    for b in range(BATCHES):
+    for b in range(1, BATCHES):
         exchange(state.at[b], state_in.at[b], state_send.at[b], state_recv.at[b])
+    for load in loads[3:]:
+        load.wait()
 
     below = lax.broadcasted_iota(jnp.int32, (E, E), 0) >= lax.broadcasted_iota(
         jnp.int32, (E, E), 1
@@ -286,6 +305,18 @@
     wait_bytes(gain_z_in.at[pl.ds(0, RING - 1)], gain_z_sems.at[0])
 
 
+def store(*refs):
+    sources, targets, sems = refs[:4], refs[4:8], refs[8]
+    copies = [
+        pltpu.make_async_copy(source, target, sems.at[i])
+        for i, (source, target) in enumerate(zip(sources, targets))
+    ]
+    for copy in copies:
+        copy.start()
+    for copy in copies:
+        copy.wait()
+
+
 def shards(queries, keys, values, forget, gain, grad_out):
     block = jax.ShapeDtypeStruct(queries.shape, BF16)
     states = pltpu.VMEM((BATCHES, CTX, 8, E), F32)
@@ -295,22 +326,39 @@
     ring = pltpu.VMEM((RING, 8, E), F32)
     pair = pltpu.SemaphoreType.DMA((2,))
     vmem = pl.BlockSpec(memory_space=pltpu.VMEM)
-    grad_q, grad_k, grad_v, grad_gain = pl.pallas_call(
+    hbm = pl.BlockSpec(memory_space=pltpu.HBM)
+    tokens = pltpu.VMEM(queries.shape, BF16)
+    shapes = (block, block, block, jax.ShapeDtypeStruct((HEADS, E), F32))
+    grads = pl.pallas_call(
         kernel,
-        out_shape=(block, block, block, jax.ShapeDtypeStruct((HEADS, E), F32)),
-        in_specs=[vmem] * 6,
+        out_shape=shapes,
+        in_specs=[hbm] * 6,
         out_specs=(vmem,) * 4,
-        scratch_shapes=[states] * 8
+        scratch_shapes=[tokens, tokens, tokens, pltpu.VMEM(forget.shape, F32), tile, tokens]
+        + [states] * 8
         + [pltpu.VMEM((GROUP, BATCHES, E), F32), pltpu.VMEM((CTX, BATCHES, E), F32)]
         + [squares_f32, squares_bf16, squares_f32, squares_bf16, squares_bf16]
         + [squares_f32, squares_f32]
         + [tile, pltpu.VMEM((TENSOR, 8, E), F32)]
         + [tile, ring, tile, ring, tile, tile]
-        + [pair] * 13,
+        + [pair] * 13
+        + [pltpu.SemaphoreType.DMA((6,))],
         compiler_params=pltpu.CompilerParams(
             collective_id=0, has_side_effects=True, vmem_limit_bytes=40 << 20
         ),
-    )(queries, keys, values, forget, gain.reshape(HEADS, E), grad_out)
+    )(
+        *(
+            pltpu.with_memory_space_constraint(x, pltpu.HBM)
+            for x in (queries, keys, values, forget, gain.reshape(HEADS, E), grad_out)
+        )
+    )
+    grad_q, grad_k, grad_v, grad_gain = pl.pallas_call(
+        store,
+        out_shape=shapes,
+        in_specs=[vmem] * 4,
+        out_specs=(hbm,) * 4,
+        scratch_shapes=[pltpu.SemaphoreType.DMA((4,))],
+    )(*grads)
     return grad_q, grad_k, grad_v, grad_gain.reshape(-1)
 
 

time: 87.8 us -> 83.4 us (0.950)
  local copies, waits for them, and re-layouts: 7.87 us -> 2.67 us
  Pallas kernels: 79 us -> 79.9 us
    unnamed x16 -> x8, local copies, waits for them, and re-layouts: 7.87 us -> 2.67 us
    pallas_call x1 -> x2, Pallas kernels: 79 us -> 79.9 us  [the longest x1 77.9 us: shards(): pl.pallas_call(kernel, out_shape=shapes, in_specs=[hbm] * 6, out_specs=(v...]
where the time goes in v2:
time: 83.4 us; the launch traced here: 83.2 us
  Pallas kernels  79.9 us (96%)
  local copies, waits for them, and re-layouts  2.67 us (3%)
    pallas_call x1, Pallas kernels, shards(): pl.pallas_call(kernel, out_shape=shapes, in_specs=[hbm] * 6, out_specs=(v...  77.9 us
    unnamed x8, local copies, waits for them, and re-layouts  2.67 us
    pallas_call x1, Pallas kernels, shards(): pl.pallas_call(store, out_shape=shapes, in_specs=[vmem] * 4, out_specs=(h...  2.02 us

profile of v2, /device:TPU:1, one launch (start us, length us, event | category | flops | bytes accessed | tf_op | source)
XLA Modules:
  0.0 83.2 jit_solution(3551510019150136065)
XLA Ops:
  0.6 77.9 %shard_map.93 = (bf16[1,128,1024]{2,1,0:T(8,128)(2,1)S(1)}, bf16[1,128,1024]{2,1,0:T(8,128)(2,1)S(1)}, bf16[1,128,1024]{2,1,0:T(8,128)(2,1)S(1)}, f32[8,128]{1,0:T(8,128)S(1)}) custom-call(bf16[1,128,1024]{2,1,0:T(8,128)(2,1)} %q_hbm.1, bf16[1,128,1024]{2,1,0:T(8,128)(2,1)} %k_hbm.1, bf16[1,128,1024]{2,1,0:T(8,128)(2,1)} %v_hbm.1, f32[1,8,128]{2,1,0:T(8,128)} %f_hbm.1, ...), custom_call_target="tpu_custom_call" | custom-call | tf_op jit(solution)/shard_map/pallas_call | solution.py:332
  78.6 0.0 copy-start
  78.6 0.7 copy-done
  79.3 0.0 copy-start.1
  79.3 0.7 copy-done.1
  79.9 0.0 copy-start.2
  79.9 0.7 copy-done.2
  80.6 0.0 copy-start.3
  80.6 0.6 copy-done.3
  81.2 2.0 %shard_map.94 = (bf16[1,128,1024]{2,1,0:T(8,128)(2,1)}, bf16[1,128,1024]{2,1,0:T(8,128)(2,1)}, bf16[1,128,1024]{2,1,0:T(8,128)(2,1)}, f32[8,128]{1,0:T(8,128)}) custom-call(bf16[1,128,1024]{2,1,0:T(8,128)(2,1)} %copy-done, bf16[1,128,1024]{2,1,0:T(8,128)(2,1)} %copy-done.1, bf16[1,128,1024]{2,1,0:T(8,128)(2,1)} %copy-done.2, f32[8,128]{1,0:T(8,128)} %copy-done.3), custom_call_target="tpu_custom_call" | custom-call | tf_op jit(solution)/shard_map/pallas_call | solution.py:355
Async XLA Ops:
  78.6 0.7 copy-start
  79.3 0.7 copy-start.1
  79.9 0.7 copy-start.2
  80.6 0.6 copy-start.3

commit v3 on v2

--- a/solution.py
+++ b/solution.py
@@ -36,6 +36,7 @@
     back, back_in, suffix, suffix_in,
     decay_out, decay_in,
     weight, weighted, attended, earlier_b, grad_att, part_k, part_v,
+    grad_normed, of_query, of_key, query_scaled,
     norm_out, norm_in,
     gain_y_out, gain_y_in, gain_z_out, gain_z_in, gain_dp_out, gain_dp_in,
     decay_sems, state_send, state_recv, prefix_send, prefix_recv,
@@ -47,8 +48,14 @@
     scale = E ** (-0.5)
     full_width = TENSOR * HEADS * E
 
+    def alternate(i):
+        half, odd = i // 2, lax.rem(i, 2)
+        return half + odd * (RING - 1 - 2 * half)
+
     def ctx_peer(i):
-        return lax.rem(z + i // RING, RING) * RING + lax.rem(y + lax.rem(i, RING), RING)
+        i = CTX - i
+        to_z, to_y = alternate(i // RING), alternate(lax.rem(i, RING))
+        return lax.rem(z + to_z, RING) * RING + lax.rem(y + to_y, RING)
 
     def tensor_peer(i):
         return lax.rem(tn + i, TENSOR)
@@ -137,10 +144,13 @@
 
     loads[1].wait()
     loads[2].wait()
-    for h in range(HEADS):
+
+    def make_state(h):
         key_scaled = (k_ref[0, :, columns(h)].astype(F32) * key_decay[:, h : h + 1]).astype(BF16)
         put_state(state, h, matmul(key_scaled, v_ref[0, :, columns(h)], 0, 0))
 
+    for h in range(GROUP):
+        make_state(h)
     pl.semaphore_wait(barrier, CTX - 1 + TENSOR - 1 + 1)
 
     def send_decay(i, carry):
@@ -154,15 +164,17 @@
     exchange(state.at[0], state_in.at[0], state_send.at[0], state_recv.at[0])
     lax.fori_loop(1, CTX, send_decay, 0)
     decay_in[me] = decay_out[me // OWNERS]
-    for b in range(1, BATCHES):
-        exchange(state.at[b], state_in.at[b], state_send.at[b], state_recv.at[b])
+    for h in range(GROUP, HEADS):
+        make_state(h)
+    exchange(state.at[1], state_in.at[1], state_send.at[1], state_recv.at[1])
     for load in loads[3:]:
         load.wait()
 
     below = lax.broadcasted_iota(jnp.int32, (E, E), 0) >= lax.broadcasted_iota(
         jnp.int32, (E, E), 1
     )
-    for h in range(HEADS):
+
+    def make_local(h):
         span = cumulative_t[:, h : h + 1] - cumulative[h : h + 1, :]
         now = jnp.where(below, jnp.exp(-jnp.where(below, span, 0.0)), 0.0)
         weight[h] = now
@@ -170,6 +182,14 @@
         rounded = (scores * scale * now).astype(BF16)
         weighted[h] = rounded
         attended[h] = matmul(rounded, v_ref[0, :, columns(h)], 1, 0)
+        grad_normed[h] = g_ref[0, :, columns(h)].astype(F32) * gain_ref[h : h + 1, :]
+        of_query[h] = jnp.broadcast_to(scale * query_decay[:, h : h + 1], (E, E))
+        of_key[h] = jnp.broadcast_to(scale * key_decay[:, h : h + 1], (E, E))
+        scaled = q_ref[0, :, columns(h)].astype(F32) * query_decay[:, h : h + 1]
+        query_scaled[h] = scaled.T.astype(BF16)
+
+    for h in range(GROUP):
+        make_local(h)
 
     others = pl.ds(0, CTX - 1)
     wait_bytes(decay_in.at[others], decay_sems.at[1])
@@ -186,6 +206,8 @@
         wait_bytes(state_in.at[b, others], state_recv.at[b])
         run_scan(b, state_in, prefix, False)
         exchange(prefix.at[b], prefix_in.at[b], prefix_send.at[b], prefix_recv.at[b])
+        for h in range(GROUP + 2 * b, GROUP + 2 * b + 2):
+            make_local(h)
 
     squares = jnp.zeros((E, E), F32)
     products = jnp.zeros((E, E), F32)
@@ -195,11 +217,10 @@
             state_b = get_state(prefix_in, h).astype(BF16)
             earlier_b[h] = state_b
             carried = matmul(q_ref[0, :, columns(h)], state_b, 1, 0)
-            now = attended[h] + scale * query_decay[:, h : h + 1] * carried
+            now = attended[h] + of_query[h] * carried
             attended[h] = now
-            grad_normed = g_ref[0, :, columns(h)].astype(F32) * gain_ref[h : h + 1, :]
             squares = squares + now * now
-            products = products + grad_normed * now
+            products = products + grad_normed[h] * now
 
     wide = lax.broadcasted_iota(jnp.int32, (E, E), 1)
     both = jnp.where(
@@ -224,20 +245,12 @@
     of_grad = jnp.broadcast_to(inverse_rms, (E, E)).T
     of_attended = jnp.broadcast_to(inverse_rms * inverse_rms * projected, (E, E)).T
 
-    for b in range(BATCHES):
+    def make_back(b):
         for h in range(b * GROUP, (b + 1) * GROUP):
-            grad_normed = g_ref[0, :, columns(h)].astype(F32) * gain_ref[h : h + 1, :]
-            grad_now = (of_grad * grad_normed - of_attended * attended[h]).astype(BF16)
+            grad_now = (of_grad * grad_normed[h] - of_attended * attended[h]).astype(BF16)
             grad_att[h] = grad_now
-            query_scaled = (
-                q_ref[0, :, columns(h)].astype(F32) * query_decay[:, h : h + 1]
-            ).astype(BF16)
-            put_state(back, h, matmul(query_scaled, grad_now, 0, 0))
+            put_state(back, h, matmul(query_scaled[h], grad_now, 1, 0))
         exchange(back.at[b], back_in.at[b], back_send.at[b], back_recv.at[b])
-
-    for h in range(HEADS):
-        normed = attended[h] * of_grad
-        gain_y_out[h] = jnp.sum(g_ref[0, :, columns(h)].astype(F32) * normed, axis=0)
 
     def sum_ring(out, into, sems, peer_of, mine):
         def go(i, carry):
@@ -254,40 +267,49 @@
             total = total + into[i]
         return total
 
+    make_back(0)
+    for h in range(HEADS):
+        normed = attended[h] * of_grad
+        gain_y_out[h] = jnp.sum(g_ref[0, :, columns(h)].astype(F32) * normed, axis=0)
     sum_ring(gain_y_out, gain_y_in, gain_y_sems, y_peer, y)
-
-    for h in range(HEADS):
+    make_back(1)
+
+    def make_parts(h):
         grad_now = grad_att[h]
         scores = matmul(grad_now, v_ref[0, :, columns(h)], 1, 1)
         grad_weighted = (scores * scale * weight[h]).astype(BF16)
-        grad_q = matmul(grad_weighted, k_ref[0, :, columns(h)], 1, 0) + scale * query_decay[
-            :, h : h + 1
-        ] * matmul(grad_now, earlier_b[h], 1, 1)
+        grad_q = matmul(grad_weighted, k_ref[0, :, columns(h)], 1, 0) + of_query[h] * matmul(
+            grad_now, earlier_b[h], 1, 1
+        )
         gq_ref[0, :, columns(h)] = grad_q.astype(BF16)
         part_k[h] = matmul(grad_weighted, q_ref[0, :, columns(h)], 0, 0)
         part_v[h] = matmul(weighted[h], grad_now, 0, 0)
 
+    for h in range(GROUP):
+        make_parts(h)
+
+    gain_z_out[...] = ring_total(gain_y_in, gain_y_sems)
+    sum_ring(gain_z_out, gain_z_in, gain_z_sems, z_peer, z)
+    other_core = remote(
+        gain_dp_out, gain_dp_in, gain_dp_sems.at[0], gain_dp_sems.at[1], (1 - dp, me, tn)
+    )
     for b in range(BATCHES):
         wait_bytes(back_in.at[b, others], back_recv.at[b])
         run_scan(b, back_in, suffix, True)
+        if b == BATCHES - 1:
+            gain_total = ring_total(gain_z_in, gain_z_sems)
+            gain_dp_out[...] = gain_total
+            other_core.start()
         exchange(suffix.at[b], suffix_in.at[b], suffix_send.at[b], suffix_recv.at[b])
-
-    gain_z_out[...] = ring_total(gain_y_in, gain_y_sems)
-    sum_ring(gain_z_out, gain_z_in, gain_z_sems, z_peer, z)
-    gain_total = ring_total(gain_z_in, gain_z_sems)
-    gain_dp_out[...] = gain_total
-    other_core = remote(
-        gain_dp_out, gain_dp_in, gain_dp_sems.at[0], gain_dp_sems.at[1], (1 - dp, me, tn)
-    )
-    other_core.start()
+        for h in range(GROUP + 2 * b, GROUP + 2 * b + 2):
+            make_parts(h)
 
     for b in range(BATCHES):
         wait_bytes(suffix_in.at[b, others], suffix_recv.at[b])
         for h in range(b * GROUP, (b + 1) * GROUP):
             later_b = get_state(suffix_in, h).astype(BF16)
-            scaling = scale * key_decay[:, h : h + 1]
-            grad_k = part_k[h] + scaling * matmul(v_ref[0, :, columns(h)], later_b, 1, 1)
-            grad_v = part_v[h] + scaling * matmul(k_ref[0, :, columns(h)], later_b, 1, 0)
+            grad_k = part_k[h] + of_key[h] * matmul(v_ref[0, :, columns(h)], later_b, 1, 1)
+            grad_v = part_v[h] + of_key[h] * matmul(k_ref[0, :, columns(h)], later_b, 1, 0)
             gk_ref[0, :, columns(h)] = grad_k.astype(BF16)
             gv_ref[0, :, columns(h)] = grad_v.astype(BF16)
 
@@ -338,7 +360,8 @@
         + [states] * 8
         + [pltpu.VMEM((GROUP, BATCHES, E), F32), pltpu.VMEM((CTX, BATCHES, E), F32)]
         + [squares_f32, squares_bf16, squares_f32, squares_bf16, squares_bf16]
-        + [squares_f32, squares_f32]
+        + [squares_f32] * 5
+        + [squares_bf16]
         + [tile, pltpu.VMEM((TENSOR, 8, E), F32)]
         + [tile, ring, tile, ring, tile, tile]
         + [pair] * 13
@@ -358,6 +381,7 @@
         in_specs=[vmem] * 4,
         out_specs=(hbm,) * 4,
         scratch_shapes=[pltpu.SemaphoreType.DMA((4,))],
+        compiler_params=pltpu.CompilerParams(vmem_limit_bytes=4 << 20),
     )(*grads)
     return grad_q, grad_k, grad_v, grad_gain.reshape(-1)
 

time: 83.4 us -> 80.5 us (0.965)
  the two profiles are of different devices: /device:TPU:1 before, /device:TPU:6 now
where the time goes in v3:
time: 80.5 us; the launch traced here: 80.4 us
  Pallas kernels  79.7 us (99%)
    pallas_call x1, Pallas kernels, shards(): pl.pallas_call(kernel, out_shape=shapes, in_specs=[hbm] * 6, out_specs=(v...  78.8 us

profile of v3, /device:TPU:6, one launch (start us, length us, event | category | flops | bytes accessed | tf_op | source)
XLA Modules:
  0.0 80.4 jit_solution(10159368042967244053)
XLA Ops:
  0.6 78.8 %shard_map.93 = (bf16[1,128,1024]{2,1,0:T(8,128)(2,1)S(1)}, bf16[1,128,1024]{2,1,0:T(8,128)(2,1)S(1)}, bf16[1,128,1024]{2,1,0:T(8,128)(2,1)S(1)}, f32[8,128]{1,0:T(8,128)S(1)}) custom-call(bf16[1,128,1024]{2,1,0:T(8,128)(2,1)} %q_hbm.1, bf16[1,128,1024]{2,1,0:T(8,128)(2,1)} %k_hbm.1, bf16[1,128,1024]{2,1,0:T(8,128)(2,1)} %v_hbm.1, f32[1,8,128]{2,1,0:T(8,128)} %f_hbm.1, ...), custom_call_target="tpu_custom_call" | custom-call | tf_op jit(solution)/shard_map/pallas_call | solution.py:354
  79.5 0.9 %shard_map.94 = (bf16[1,128,1024]{2,1,0:T(8,128)(2,1)}, bf16[1,128,1024]{2,1,0:T(8,128)(2,1)}, bf16[1,128,1024]{2,1,0:T(8,128)(2,1)}, f32[8,128]{1,0:T(8,128)}) custom-call(bf16[1,128,1024]{2,1,0:T(8,128)(2,1)S(1)} %get-tuple-element.12.refs_0_, bf16[1,128,1024]{2,1,0:T(8,128)(2,1)S(1)} %get-tuple-element.13.refs_1_, ...), custom_call_target="tpu_custom_call" | custom-call | tf_op jit(solution)/shard_map/pallas_call | solution.py:378

commit v4 on v3

--- a/solution.py
+++ b/solution.py
@@ -18,6 +18,7 @@
 RING = 8
 TENSOR = 4
 BATCHES = 2
+STAGGER = 2
 GROUP = HEADS // BATCHES
 OWNERS = CTX // GROUP
 
@@ -41,7 +42,7 @@
     gain_y_out, gain_y_in, gain_z_out, gain_z_in, gain_dp_out, gain_dp_in,
     decay_sems, state_send, state_recv, prefix_send, prefix_recv,
     back_send, back_recv, suffix_send, suffix_recv,
-    norm_sems, gain_y_sems, gain_z_sems, gain_dp_sems, load_sems,
+    norm_sems, gain_y_sems, gain_z_sems, gain_dp_sems, load_sems, turn_sem,
 ):
     dp, me, tn = lax.axis_index("dp"), lax.axis_index("ctx"), lax.axis_index("tensor")
     z, y = me // RING, lax.rem(me, RING)
@@ -161,6 +162,10 @@
         ).start()
         return carry
 
+    @pl.when(dp == 1)
+    def _():
+        pl.semaphore_wait(turn_sem, 1)
+
     exchange(state.at[0], state_in.at[0], state_send.at[0], state_recv.at[0])
     lax.fori_loop(1, CTX, send_decay, 0)
     decay_in[me] = decay_out[me // OWNERS]
@@ -192,6 +197,13 @@
         make_local(h)
 
     others = pl.ds(0, CTX - 1)
+    for b in range(STAGGER):
+        wait_bytes(state.at[b, others], state_send.at[b])
+
+    @pl.when(dp == 0)
+    def _():
+        pl.semaphore_signal(turn_sem, inc=1, device_id=(1, me, tn), device_id_type=MESH)
+
     wait_bytes(decay_in.at[others], decay_sems.at[1])
 
     def run_scan(b, source, result, reverse):
@@ -317,8 +329,9 @@
     gg_ref[...] = gain_total + gain_dp_in[...]
 
     wait_bytes(decay_in.at[others], decay_sems.at[0])
+    for b in range(STAGGER, BATCHES):
+        wait_bytes(state.at[b, others], state_send.at[b])
     for b in range(BATCHES):
-        wait_bytes(state.at[b, others], state_send.at[b])
         wait_bytes(prefix.at[b, others], prefix_send.at[b])
         wait_bytes(back.at[b, others], back_send.at[b])
         wait_bytes(suffix.at[b, others], suffix_send.at[b])
@@ -365,7 +378,7 @@
         + [tile, pltpu.VMEM((TENSOR, 8, E), F32)]
         + [tile, ring, tile, ring, tile, tile]
         + [pair] * 13
-        + [pltpu.SemaphoreType.DMA((6,))],
+        + [pltpu.SemaphoreType.DMA((6,)), pltpu.SemaphoreType.REGULAR],
         compiler_params=pltpu.CompilerParams(
             collective_id=0, has_side_effects=True, vmem_limit_bytes=40 << 20
         ),

time: 80.5 us -> 79.5 us (0.988)
  the two profiles are of different devices: /device:TPU:6 before, /device:TPU:1 now
where the time goes in v4:
time: 79.5 us; the launch traced here: 79.4 us
  Pallas kernels  78.8 us (99%)
    pallas_call x1, Pallas kernels, shards(): pl.pallas_call(kernel, out_shape=shapes, in_specs=[hbm] * 6, out_specs=(v...  77.8 us

profile of v4, /device:TPU:1, one launch (start us, length us, event | category | flops | bytes accessed | tf_op | source)
XLA Modules:
  0.0 79.4 jit_solution(9168487749187439868)
XLA Ops:
  0.6 77.8 %shard_map.93 = (bf16[1,128,1024]{2,1,0:T(8,128)(2,1)S(1)}, bf16[1,128,1024]{2,1,0:T(8,128)(2,1)S(1)}, bf16[1,128,1024]{2,1,0:T(8,128)(2,1)S(1)}, f32[8,128]{1,0:T(8,128)S(1)}) custom-call(bf16[1,128,1024]{2,1,0:T(8,128)(2,1)} %q_hbm.1, bf16[1,128,1024]{2,1,0:T(8,128)(2,1)} %k_hbm.1, bf16[1,128,1024]{2,1,0:T(8,128)(2,1)} %v_hbm.1, f32[1,8,128]{2,1,0:T(8,128)} %f_hbm.1, ...), custom_call_target="tpu_custom_call" | custom-call | tf_op jit(solution)/shard_map/pallas_call | solution.py:367
  78.5 0.9 %shard_map.94 = (bf16[1,128,1024]{2,1,0:T(8,128)(2,1)}, bf16[1,128,1024]{2,1,0:T(8,128)(2,1)}, bf16[1,128,1024]{2,1,0:T(8,128)(2,1)}, f32[8,128]{1,0:T(8,128)}) custom-call(bf16[1,128,1024]{2,1,0:T(8,128)(2,1)S(1)} %get-tuple-element.12.refs_0_, bf16[1,128,1024]{2,1,0:T(8,128)(2,1)S(1)} %get-tuple-element.13.refs_1_, ...), custom_call_target="tpu_custom_call" | custom-call | tf_op jit(solution)/shard_map/pallas_call | solution.py:391

commit v5 on v3

--- a/solution.py
+++ b/solution.py
@@ -14,12 +14,13 @@
 BF16 = jnp.bfloat16
 
 HEADS = 8
-CTX = 64
 RING = 8
 TENSOR = 4
-BATCHES = 2
+BATCHES = 4
 GROUP = HEADS // BATCHES
-OWNERS = CTX // GROUP
+SPLIT = RING // GROUP
+ROWS = E // SPLIT
+FULL = pl.ds(0, ROWS + 1)
 
 
 def matmul(a, b, contract_a, contract_b):
@@ -32,30 +33,20 @@
     q_hbm, k_hbm, v_hbm, f_hbm, gain_hbm, g_hbm,
     gq_ref, gk_ref, gv_ref, gg_ref,
     q_ref, k_ref, v_ref, f_ref, gain_ref, g_ref,
-    state, state_in, prefix, prefix_in,
-    back, back_in, suffix, suffix_in,
-    decay_out, decay_in,
+    state, state_in, row_out, row_in, prefix, prefix_in,
+    back, back_in, row_back_out, row_back_in, suffix, suffix_in,
     weight, weighted, attended, earlier_b, grad_att, part_k, part_v,
     grad_normed, of_query, of_key, query_scaled,
     norm_out, norm_in,
     gain_y_out, gain_y_in, gain_z_out, gain_z_in, gain_dp_out, gain_dp_in,
-    decay_sems, state_send, state_recv, prefix_send, prefix_recv,
-    back_send, back_recv, suffix_send, suffix_recv,
+    state_send, state_recv, row_send, row_recv, prefix_send, prefix_recv,
+    back_send, back_recv, row_back_send, row_back_recv, suffix_send, suffix_recv,
     norm_sems, gain_y_sems, gain_z_sems, gain_dp_sems, load_sems,
 ):
     dp, me, tn = lax.axis_index("dp"), lax.axis_index("ctx"), lax.axis_index("tensor")
     z, y = me // RING, lax.rem(me, RING)
     scale = E ** (-0.5)
     full_width = TENSOR * HEADS * E
-
-    def alternate(i):
-        half, odd = i // 2, lax.rem(i, 2)
-        return half + odd * (RING - 1 - 2 * half)
-
-    def ctx_peer(i):
-        i = CTX - i
-        to_z, to_y = alternate(i // RING), alternate(lax.rem(i, RING))
-        return lax.rem(z + to_z, RING) * RING + lax.rem(y + to_y, RING)
 
     def tensor_peer(i):
         return lax.rem(tn + i, TENSOR)
@@ -80,21 +71,15 @@
 
     barrier = pltpu.get_barrier_semaphore()
 
-    def greet_ctx(i, carry):
-        pl.semaphore_signal(
-            barrier, inc=1, device_id=(dp, ctx_peer(i), tn), device_id_type=MESH
-        )
-        return carry
-
-    def greet_tensor(i, carry):
+    for i in range(1, RING):
+        for peer in (y_peer(i), z_peer(i)):
+            pl.semaphore_signal(barrier, inc=1, device_id=(dp, peer, tn), device_id_type=MESH)
+    for i in range(1, TENSOR):
         pl.semaphore_signal(
             barrier, inc=1, device_id=(dp, me, tensor_peer(i)), device_id_type=MESH
         )
-        return carry
-
-    lax.fori_loop(1, CTX, greet_ctx, 0)
-    lax.fori_loop(1, TENSOR, greet_tensor, 0)
     pl.semaphore_signal(barrier, inc=1, device_id=(1 - dp, me, tn), device_id_type=MESH)
+    greeted = 2 * (RING - 1) + TENSOR - 1 + 1
 
     def remote(src, dst, send_sem, recv_sem, device):
         return pltpu.make_async_remote_copy(
@@ -105,14 +90,68 @@
     def wait_bytes(ref, sem):
         pltpu.make_async_copy(ref, ref, sem).wait()
 
-    def exchange(src, dst, send_sem, recv_sem):
-        def go(i, carry):
-            peer = ctx_peer(i)
-            remote(src.at[peer], dst.at[me], send_sem, recv_sem, (dp, peer, tn)).start()
-            return carry
-
-        lax.fori_loop(1, CTX, go, 0)
-        dst[me] = src[me]
+    others = pl.ds(0, RING - 1)
+    far_first = (4, 3, 5, 2, 6, 1, 7)
+
+    def exchange(src, dst, send_sem, recv_sem, rows):
+        for i in far_first:
+            peer = lax.rem(y + i, RING)
+            remote(
+                src.at[peer, rows], dst.at[y, rows], send_sem, recv_sem,
+                (dp, z * RING + peer, tn),
+            ).start()
+        dst[y, rows] = src[y, rows]
+
+    def row_peers(later):
+        for i in range(RING - 1, 0, -1):
+            peer = z + i if later else z - i
+            yield i, peer, (peer < RING) if later else (peer >= 0)
+
+    def send_row(out, into, send_sems, recv_sems, later):
+        for i, peer, exists in row_peers(later):
+
+            @pl.when(exists)
+            def _(i=i, peer=peer):
+                remote(
+                    out.at[FULL], into.at[z, FULL], send_sems.at[i], recv_sems.at[z],
+                    (dp, peer * RING + y, tn),
+                ).start()
+
+    def row_sent(out, send_sems, later):
+        for i, _, exists in row_peers(later):
+
+            @pl.when(exists)
+            def _(i=i):
+                wait_bytes(out.at[FULL], send_sems.at[i])
+
+    def row_arrived(into, recv_sems, later):
+        for i, peer, exists in row_peers(not later):
+
+            @pl.when(exists)
+            def _(peer=peer):
+                wait_bytes(into.at[peer, FULL], recv_sems.at[peer])
+
+    def row_total(source, out, reverse):
+        total = jnp.zeros((ROWS, E), F32)
+        decay = jnp.ones((1, E), F32)
+        for at in range(RING - 1, -1, -1) if reverse else range(RING):
+            passing = source[at, ROWS : ROWS + 1]
+            total = total * passing + source[at, 0:ROWS]
+            decay = decay * passing
+        out[0:ROWS] = total
+        out[ROWS : ROWS + 1] = decay
+
+    def run_scan(source, rows, result, reverse):
+        def of_row(i, total):
+            at = RING - 1 - i if reverse else i
+            return total * rows[at, ROWS : ROWS + 1] + rows[at, 0:ROWS]
+
+        total = lax.fori_loop(
+            0, RING - 1 - z if reverse else z, of_row, jnp.zeros((ROWS, E), F32)
+        )
+        for at in range(RING - 1, -1, -1) if reverse else range(RING):
+            result[at] = total
+            total = total * source[at, ROWS : ROWS + 1] + source[at, 0:ROWS]
 
     loads[0].wait()
     lanes = lax.broadcasted_iota(jnp.int32, (HEADS, E), 1)
@@ -122,8 +161,6 @@
         cumulative = cumulative + jnp.where(lanes >= shift, moved, 0.0)
     block_decay = cumulative[:, E - 1 :]
     passing = jnp.broadcast_to(jnp.exp(-block_decay), (HEADS, E))
-    for h in range(HEADS):
-        decay_out[h % GROUP, h // GROUP] = passing[h]
     cumulative_t = cumulative.T
     query_decay = jnp.exp(-cumulative).T
     key_decay = jnp.exp(-(block_decay - cumulative)).T
@@ -132,15 +169,16 @@
         return slice(h * E, (h + 1) * E)
 
     def pieces(h):
-        return h // GROUP, slice((h % GROUP) * OWNERS, (h % GROUP + 1) * OWNERS)
+        return h // GROUP, slice((h % GROUP) * SPLIT, (h % GROUP + 1) * SPLIT)
 
     def put_state(ref, h, value):
-        batch, rows = pieces(h)
-        ref[batch, rows] = value.reshape(OWNERS, 8, E)
+        batch, owners = pieces(h)
+        ref[batch, owners, 0:ROWS] = value.reshape(SPLIT, ROWS, E)
+        ref[batch, owners, ROWS : ROWS + 1] = jnp.broadcast_to(passing[h], (SPLIT, 1, E))
 
     def get_state(ref, h):
-        batch, rows = pieces(h)
-        return ref[batch, rows].reshape(E, E)
+        batch, owners = pieces(h)
+        return ref[batch, owners].reshape(E, E)
 
     loads[1].wait()
     loads[2].wait()
@@ -149,24 +187,11 @@
         key_scaled = (k_ref[0, :, columns(h)].astype(F32) * key_decay[:, h : h + 1]).astype(BF16)
         put_state(state, h, matmul(key_scaled, v_ref[0, :, columns(h)], 0, 0))
 
-    for h in range(GROUP):
+    for h in range(HEADS):
         make_state(h)
-    pl.semaphore_wait(barrier, CTX - 1 + TENSOR - 1 + 1)
-
-    def send_decay(i, carry):
-        peer = ctx_peer(i)
-        remote(
-            decay_out.at[peer // OWNERS], decay_in.at[me],
-            decay_sems.at[0], decay_sems.at[1], (dp, peer, tn),
-        ).start()
-        return carry
-
-    exchange(state.at[0], state_in.at[0], state_send.at[0], state_recv.at[0])
-    lax.fori_loop(1, CTX, send_decay, 0)
-    decay_in[me] = decay_out[me // OWNERS]
-    for h in range(GROUP, HEADS):
-        make_state(h)
-    exchange(state.at[1], state_in.at[1], state_send.at[1], state_recv.at[1])
+    pl.semaphore_wait(barrier, greeted)
+    for b in range(BATCHES):
+        exchange(state.at[b], state_in.at[b], state_send.at[b], state_recv.at[b], FULL)
     for load in loads[3:]:
         load.wait()
 
@@ -188,26 +213,18 @@
         scaled = q_ref[0, :, columns(h)].astype(F32) * query_decay[:, h : h + 1]
         query_scaled[h] = scaled.T.astype(BF16)
 
-    for h in range(GROUP):
+    for h in range(HEADS):
         make_local(h)
-
-    others = pl.ds(0, CTX - 1)
-    wait_bytes(decay_in.at[others], decay_sems.at[1])
-
-    def run_scan(b, source, result, reverse):
-        def step(i, total):
-            at = CTX - 1 - i if reverse else i
-            result[b, at] = total
-            return total * decay_in[at, b : b + 1] + source[b, at]
-
-        lax.fori_loop(0, CTX, step, jnp.zeros((8, E), F32), unroll=8)
-
-    for b in range(BATCHES):
-        wait_bytes(state_in.at[b, others], state_recv.at[b])
-        run_scan(b, state_in, prefix, False)
-        exchange(prefix.at[b], prefix_in.at[b], prefix_send.at[b], prefix_recv.at[b])
-        for h in range(GROUP + 2 * b, GROUP + 2 * b + 2):
-            make_local(h)
+    for b in range(BATCHES):
+        wait_bytes(state_in.at[b, others, FULL], state_recv.at[b])
+        row_total(state_in.at[b], row_out.at[b], False)
+        send_row(row_out.at[b], row_in.at[b], row_send.at[b], row_recv.at[b], True)
+    for b in range(BATCHES):
+        row_arrived(row_in.at[b], row_recv.at[b], True)
+        run_scan(state_in.at[b], row_in.at[b], prefix.at[b], False)
+        exchange(
+            prefix.at[b], prefix_in.at[b], prefix_send.at[b], prefix_recv.at[b], pl.ds(0, ROWS)
+        )
 
     squares = jnp.zeros((E, E), F32)
     products = jnp.zeros((E, E), F32)
@@ -250,7 +267,7 @@
             grad_now = (of_grad * grad_normed[h] - of_attended * attended[h]).astype(BF16)
             grad_att[h] = grad_now
             put_state(back, h, matmul(query_scaled[h], grad_now, 1, 0))
-        exchange(back.at[b], back_in.at[b], back_send.at[b], back_recv.at[b])
+        exchange(back.at[b], back_in.at[b], back_send.at[b], back_recv.at[b], FULL)
 
     def sum_ring(out, into, sems, peer_of, mine):
         def go(i, carry):
@@ -267,12 +284,12 @@
             total = total + into[i]
         return total
 
-    make_back(0)
+    for b in range(BATCHES):
+        make_back(b)
     for h in range(HEADS):
         normed = attended[h] * of_grad
         gain_y_out[h] = jnp.sum(g_ref[0, :, columns(h)].astype(F32) * normed, axis=0)
     sum_ring(gain_y_out, gain_y_in, gain_y_sems, y_peer, y)
-    make_back(1)
 
     def make_parts(h):
         grad_now = grad_att[h]
@@ -285,25 +302,28 @@
         part_k[h] = matmul(grad_weighted, q_ref[0, :, columns(h)], 0, 0)
         part_v[h] = matmul(weighted[h], grad_now, 0, 0)
 
-    for h in range(GROUP):
+    for h in range(HEADS):
         make_parts(h)
-
+    for b in range(BATCHES):
+        wait_bytes(back_in.at[b, others, FULL], back_recv.at[b])
+        row_total(back_in.at[b], row_back_out.at[b], True)
+        send_row(
+            row_back_out.at[b], row_back_in.at[b], row_back_send.at[b], row_back_recv.at[b], False
+        )
     gain_z_out[...] = ring_total(gain_y_in, gain_y_sems)
     sum_ring(gain_z_out, gain_z_in, gain_z_sems, z_peer, z)
+    for b in range(BATCHES):
+        row_arrived(row_back_in.at[b], row_back_recv.at[b], False)
+        run_scan(back_in.at[b], row_back_in.at[b], suffix.at[b], True)
+        exchange(
+            suffix.at[b], suffix_in.at[b], suffix_send.at[b], suffix_recv.at[b], pl.ds(0, ROWS)
+        )
+    gain_total = ring_total(gain_z_in, gain_z_sems)
+    gain_dp_out[...] = gain_total
     other_core = remote(
         gain_dp_out, gain_dp_in, gain_dp_sems.at[0], gain_dp_sems.at[1], (1 - dp, me, tn)
     )
-    for b in range(BATCHES):
-        wait_bytes(back_in.at[b, others], back_recv.at[b])
-        run_scan(b, back_in, suffix, True)
-        if b == BATCHES - 1:
-            gain_total = ring_total(gain_z_in, gain_z_sems)
-            gain_dp_out[...] = gain_total
-            other_core.start()
-        exchange(suffix.at[b], suffix_in.at[b], suffix_send.at[b], suffix_recv.at[b])
-        for h in range(GROUP + 2 * b, GROUP + 2 * b + 2):
-            make_parts(h)
-
+    other_core.start()
     for b in range(BATCHES):
         wait_bytes(suffix_in.at[b, others], suffix_recv.at[b])
         for h in range(b * GROUP, (b + 1) * GROUP):
@@ -316,11 +336,12 @@
     other_core.wait()
     gg_ref[...] = gain_total + gain_dp_in[...]
 
-    wait_bytes(decay_in.at[others], decay_sems.at[0])
-    for b in range(BATCHES):
-        wait_bytes(state.at[b, others], state_send.at[b])
+    for b in range(BATCHES):
+        wait_bytes(state.at[b, others, FULL], state_send.at[b])
+        row_sent(row_out.at[b], row_send.at[b], True)
         wait_bytes(prefix.at[b, others], prefix_send.at[b])
-        wait_bytes(back.at[b, others], back_send.at[b])
+        wait_bytes(back.at[b, others, FULL], back_send.at[b])
+        row_sent(row_back_out.at[b], row_back_send.at[b], False)
         wait_bytes(suffix.at[b, others], suffix_send.at[b])
     wait_bytes(norm_in.at[pl.ds(0, TENSOR - 1)], norm_sems.at[0])
     wait_bytes(gain_y_in.at[pl.ds(0, RING - 1)], gain_y_sems.at[0])
@@ -341,12 +362,18 @@
 
 def shards(queries, keys, values, forget, gain, grad_out):
     block = jax.ShapeDtypeStruct(queries.shape, BF16)
-    states = pltpu.VMEM((BATCHES, CTX, 8, E), F32)
+    rows = pltpu.VMEM((BATCHES, RING, ROWS, E), F32)
+    rows_more = pltpu.VMEM((BATCHES, RING, ROWS + 8, E), F32)
+    total = pltpu.VMEM((BATCHES, ROWS + 8, E), F32)
+    one_scan = [rows_more, rows_more, total, rows_more, rows, rows]
     squares_f32 = pltpu.VMEM((HEADS, E, E), F32)
     squares_bf16 = pltpu.VMEM((HEADS, E, E), BF16)
     tile = pltpu.VMEM((8, E), F32)
     ring = pltpu.VMEM((RING, 8, E), F32)
     pair = pltpu.SemaphoreType.DMA((2,))
+    each = pltpu.SemaphoreType.DMA((BATCHES,))
+    each_row = pltpu.SemaphoreType.DMA((BATCHES, RING))
+    scan_sems = [each, each, each_row, each_row, each, each]
     vmem = pl.BlockSpec(memory_space=pltpu.VMEM)
     hbm = pl.BlockSpec(memory_space=pltpu.HBM)
     tokens = pltpu.VMEM(queries.shape, BF16)
@@ -357,14 +384,14 @@
         in_specs=[hbm] * 6,
         out_specs=(vmem,) * 4,
         scratch_shapes=[tokens, tokens, tokens, pltpu.VMEM(forget.shape, F32), tile, tokens]
-        + [states] * 8
-        + [pltpu.VMEM((GROUP, BATCHES, E), F32), pltpu.VMEM((CTX, BATCHES, E), F32)]
+        + one_scan * 2
         + [squares_f32, squares_bf16, squares_f32, squares_bf16, squares_bf16]
         + [squares_f32] * 5
         + [squares_bf16]
         + [tile, pltpu.VMEM((TENSOR, 8, E), F32)]
         + [tile, ring, tile, ring, tile, tile]
-        + [pair] * 13
+        + scan_sems * 2
+        + [pair] * 4
         + [pltpu.SemaphoreType.DMA((6,))],
         compiler_params=pltpu.CompilerParams(
             collective_id=0, has_side_effects=True, vmem_limit_bytes=40 << 20

time: 80.5 us -> 72.7 us (0.903)
  the two profiles are of different devices: /device:TPU:6 before, /device:TPU:8 now
where the time goes in v5:
time: 72.7 us; the launch traced here: 72.6 us
  Pallas kernels  72 us (99%)
    pallas_call x1, Pallas kernels, shards(): pl.pallas_call(kernel, out_shape=shapes, in_specs=[hbm] * 6, out_specs=(v...  71.1 us

profile of v5, /device:TPU:8, one launch (start us, length us, event | category | flops | bytes accessed | tf_op | source)
XLA Modules:
  0.0 72.6 jit_solution(9883052496953324697)
XLA Ops:
  0.6 71.1 %shard_map.93 = (bf16[1,128,1024]{2,1,0:T(8,128)(2,1)S(1)}, bf16[1,128,1024]{2,1,0:T(8,128)(2,1)S(1)}, bf16[1,128,1024]{2,1,0:T(8,128)(2,1)S(1)}, f32[8,128]{1,0:T(8,128)S(1)}) custom-call(bf16[1,128,1024]{2,1,0:T(8,128)(2,1)} %q_hbm.1, bf16[1,128,1024]{2,1,0:T(8,128)(2,1)} %k_hbm.1, bf16[1,128,1024]{2,1,0:T(8,128)(2,1)} %v_hbm.1, f32[1,8,128]{2,1,0:T(8,128)} %f_hbm.1, ...), custom_call_target="tpu_custom_call" | custom-call | tf_op jit(solution)/shard_map/pallas_call | solution.py:381
  71.7 0.9 %shard_map.94 = (bf16[1,128,1024]{2,1,0:T(8,128)(2,1)}, bf16[1,128,1024]{2,1,0:T(8,128)(2,1)}, bf16[1,128,1024]{2,1,0:T(8,128)(2,1)}, f32[8,128]{1,0:T(8,128)}) custom-call(bf16[1,128,1024]{2,1,0:T(8,128)(2,1)S(1)} %get-tuple-element.12.refs_0_, bf16[1,128,1024]{2,1,0:T(8,128)(2,1)S(1)} %get-tuple-element.13.refs_1_, ...), custom_call_target="tpu_custom_call" | custom-call | tf_op jit(solution)/shard_map/pallas_call | solution.py:405

commit v6 on v5

--- a/solution.py
+++ b/solution.py
@@ -15,11 +15,13 @@
 
 HEADS = 8
 RING = 8
+FAR_FIRST = (4, 3, 5, 2, 6, 1, 7)
 TENSOR = 4
 BATCHES = 4
 GROUP = HEADS // BATCHES
 SPLIT = RING // GROUP
 ROWS = E // SPLIT
+PART = pl.ds(0, ROWS)
 FULL = pl.ds(0, ROWS + 1)
 
 
@@ -57,6 +59,18 @@
     def z_peer(i):
         return lax.rem(z + i, RING) * RING + y
 
+    barrier = pltpu.get_barrier_semaphore()
+
+    for i in FAR_FIRST:
+        for peer in (y_peer(i), z_peer(i)):
+            pl.semaphore_signal(barrier, inc=1, device_id=(dp, peer, tn), device_id_type=MESH)
+    for i in range(1, TENSOR):
+        pl.semaphore_signal(
+            barrier, inc=1, device_id=(dp, me, tensor_peer(i)), device_id_type=MESH
+        )
+    pl.semaphore_signal(barrier, inc=1, device_id=(1 - dp, me, tn), device_id_type=MESH)
+    greeted = 2 * (RING - 1) + TENSOR - 1 + 1
+
     loads = [
         pltpu.make_async_copy(source, target, load_sems.at[i])
         for i, (source, target) in enumerate(
@@ -69,18 +83,6 @@
     for load in loads:
         load.start()
 
-    barrier = pltpu.get_barrier_semaphore()
-
-    for i in range(1, RING):
-        for peer in (y_peer(i), z_peer(i)):
-            pl.semaphore_signal(barrier, inc=1, device_id=(dp, peer, tn), device_id_type=MESH)
-    for i in range(1, TENSOR):
-        pl.semaphore_signal(
-            barrier, inc=1, device_id=(dp, me, tensor_peer(i)), device_id_type=MESH
-        )
-    pl.semaphore_signal(barrier, inc=1, device_id=(1 - dp, me, tn), device_id_type=MESH)
-    greeted = 2 * (RING - 1) + TENSOR - 1 + 1
-
     def remote(src, dst, send_sem, recv_sem, device):
         return pltpu.make_async_remote_copy(
             src_ref=src, dst_ref=dst, send_sem=send_sem, recv_sem=recv_sem,
@@ -91,11 +93,10 @@
         pltpu.make_async_copy(ref, ref, sem).wait()
 
     others = pl.ds(0, RING - 1)
-    far_first = (4, 3, 5, 2, 6, 1, 7)
 
     def exchange(src, dst, send_sem, recv_sem, rows):
-        for i in far_first:
-            peer = lax.rem(y + i, RING)
+        for i in FAR_FIRST:
+            peer = lax.rem(y + jnp.where(dp == 0, i, RING - i), RING)
             remote(
                 src.at[peer, rows], dst.at[y, rows], send_sem, recv_sem,
                 (dp, z * RING + peer, tn),
@@ -103,7 +104,7 @@
         dst[y, rows] = src[y, rows]
 
     def row_peers(later):
-        for i in range(RING - 1, 0, -1):
+        for i in FAR_FIRST:
             peer = z + i if later else z - i
             yield i, peer, (peer < RING) if later else (peer >= 0)
 
@@ -131,17 +132,17 @@
             def _(peer=peer):
                 wait_bytes(into.at[peer, FULL], recv_sems.at[peer])
 
-    def row_total(source, out, reverse):
+    def row_total(source, decays, out, reverse):
         total = jnp.zeros((ROWS, E), F32)
         decay = jnp.ones((1, E), F32)
         for at in range(RING - 1, -1, -1) if reverse else range(RING):
-            passing = source[at, ROWS : ROWS + 1]
-            total = total * passing + source[at, 0:ROWS]
-            decay = decay * passing
+            passed = decays[at, ROWS : ROWS + 1]
+            total = total * passed + source[at]
+            decay = decay * passed
         out[0:ROWS] = total
         out[ROWS : ROWS + 1] = decay
 
-    def run_scan(source, rows, result, reverse):
+    def run_scan(source, decays, rows, result, reverse):
         def of_row(i, total):
             at = RING - 1 - i if reverse else i
             return total * rows[at, ROWS : ROWS + 1] + rows[at, 0:ROWS]
@@ -151,7 +152,7 @@
         )
         for at in range(RING - 1, -1, -1) if reverse else range(RING):
             result[at] = total
-            total = total * source[at, ROWS : ROWS + 1] + source[at, 0:ROWS]
+            total = total * decays[at, ROWS : ROWS + 1] + source[at]
 
     loads[0].wait()
     lanes = lax.broadcasted_iota(jnp.int32, (HEADS, E), 1)
@@ -174,7 +175,6 @@
     def put_state(ref, h, value):
         batch, owners = pieces(h)
         ref[batch, owners, 0:ROWS] = value.reshape(SPLIT, ROWS, E)
-        ref[batch, owners, ROWS : ROWS + 1] = jnp.broadcast_to(passing[h], (SPLIT, 1, E))
 
     def get_state(ref, h):
         batch, owners = pieces(h)
@@ -186,6 +186,8 @@
     def make_state(h):
         key_scaled = (k_ref[0, :, columns(h)].astype(F32) * key_decay[:, h : h + 1]).astype(BF16)
         put_state(state, h, matmul(key_scaled, v_ref[0, :, columns(h)], 0, 0))
+        batch, owners = pieces(h)
+        state[batch, owners, ROWS : ROWS + 1] = jnp.broadcast_to(passing[h], (SPLIT, 1, E))
 
     for h in range(HEADS):
         make_state(h)
@@ -217,13 +219,13 @@
         make_local(h)
     for b in range(BATCHES):
         wait_bytes(state_in.at[b, others, FULL], state_recv.at[b])
-        row_total(state_in.at[b], row_out.at[b], False)
+        row_total(state_in.at[b, :, 0:ROWS], state_in.at[b], row_out.at[b], False)
         send_row(row_out.at[b], row_in.at[b], row_send.at[b], row_recv.at[b], True)
     for b in range(BATCHES):
         row_arrived(row_in.at[b], row_recv.at[b], True)
-        run_scan(state_in.at[b], row_in.at[b], prefix.at[b], False)
+        run_scan(state_in.at[b, :, 0:ROWS], state_in.at[b], row_in.at[b], prefix.at[b], False)
         exchange(
-            prefix.at[b], prefix_in.at[b], prefix_send.at[b], prefix_recv.at[b], pl.ds(0, ROWS)
+            prefix.at[b], prefix_in.at[b], prefix_send.at[b], prefix_recv.at[b], PART
         )
 
     squares = jnp.zeros((E, E), F32)
@@ -267,7 +269,7 @@
             grad_now = (of_grad * grad_normed[h] - of_attended * attended[h]).astype(BF16)
             grad_att[h] = grad_now
             put_state(back, h, matmul(query_scaled[h], grad_now, 1, 0))
-        exchange(back.at[b], back_in.at[b], back_send.at[b], back_recv.at[b], FULL)
+        exchange(back.at[b], back_in.at[b], back_send.at[b], back_recv.at[b], PART)
 
     def sum_ring(out, into, sems, peer_of, mine):
         def go(i, carry):
@@ -305,8 +307,8 @@
     for h in range(HEADS):
         make_parts(h)
     for b in range(BATCHES):
-        wait_bytes(back_in.at[b, others, FULL], back_recv.at[b])
-        row_total(back_in.at[b], row_back_out.at[b], True)
+        wait_bytes(back_in.at[b, others], back_recv.at[b])
+        row_total(back_in.at[b], state_in.at[b], row_back_out.at[b], True)
         send_row(
             row_back_out.at[b], row_back_in.at[b], row_back_send.at[b], row_back_recv.at[b], False
         )
@@ -314,9 +316,9 @@
     sum_ring(gain_z_out, gain_z_in, gain_z_sems, z_peer, z)
     for b in range(BATCHES):
         row_arrived(row_back_in.at[b], row_back_recv.at[b], False)
-        run_scan(back_in.at[b], row_back_in.at[b], suffix.at[b], True)
+        run_scan(back_in.at[b], state_in.at[b], row_back_in.at[b], suffix.at[b], True)
         exchange(
-            suffix.at[b], suffix_in.at[b], suffix_send.at[b], suffix_recv.at[b], pl.ds(0, ROWS)
+            suffix.at[b], suffix_in.at[b], suffix_send.at[b], suffix_recv.at[b], PART
         )
     gain_total = ring_total(gain_z_in, gain_z_sems)
     gain_dp_out[...] = gain_total
@@ -340,7 +342,7 @@
         wait_bytes(state.at[b, others, FULL], state_send.at[b])
         row_sent(row_out.at[b], row_send.at[b], True)
         wait_bytes(prefix.at[b, others], prefix_send.at[b])
-        wait_bytes(back.at[b, others, FULL], back_send.at[b])
+        wait_bytes(back.at[b, others], back_send.at[b])
         row_sent(row_back_out.at[b], row_back_send.at[b], False)
         wait_bytes(suffix.at[b, others], suffix_send.at[b])
     wait_bytes(norm_in.at[pl.ds(0, TENSOR - 1)], norm_sems.at[0])
@@ -365,7 +367,8 @@
     rows = pltpu.VMEM((BATCHES, RING, ROWS, E), F32)
     rows_more = pltpu.VMEM((BATCHES, RING, ROWS + 8, E), F32)
     total = pltpu.VMEM((BATCHES, ROWS + 8, E), F32)
-    one_scan = [rows_more, rows_more, total, rows_more, rows, rows]
+    first = [rows_more, rows_more, total, rows_more, rows, rows]
+    second = [rows, rows, total, rows_more, rows, rows]
     squares_f32 = pltpu.VMEM((HEADS, E, E), F32)
     squares_bf16 = pltpu.VMEM((HEADS, E, E), BF16)
     tile = pltpu.VMEM((8, E), F32)
@@ -384,7 +387,8 @@
         in_specs=[hbm] * 6,
         out_specs=(vmem,) * 4,
         scratch_shapes=[tokens, tokens, tokens, pltpu.VMEM(forget.shape, F32), tile, tokens]
-        + one_scan * 2
+        + first
+        + second
         + [squares_f32, squares_bf16, squares_f32, squares_bf16, squares_bf16]
         + [squares_f32] * 5
         + [squares_bf16]

time: 72.7 us -> 74.4 us (1.023)
  Pallas kernels: 72 us -> 73.6 us
    pallas_call x1, Pallas kernels: 71.1 us -> 72.7 us  [shards(): pl.pallas_call(kernel, out_shape=shapes, in_specs=[hbm] * 6, out_specs=(v...]
where the time goes in v6:
time: 74.4 us; the launch traced here: 74.3 us
  Pallas kernels  73.6 us (99%)
    pallas_call x1, Pallas kernels, shards(): pl.pallas_call(kernel, out_shape=shapes, in_specs=[hbm] * 6, out_specs=(v...  72.7 us

profile of v6, /device:TPU:8, one launch (start us, length us, event | category | flops | bytes accessed | tf_op | source)
XLA Modules:
  0.0 74.3 jit_solution(13182182802833223878)
XLA Ops:
  0.6 72.7 %shard_map.93 = (bf16[1,128,1024]{2,1,0:T(8,128)(2,1)S(1)}, bf16[1,128,1024]{2,1,0:T(8,128)(2,1)S(1)}, bf16[1,128,1024]{2,1,0:T(8,128)(2,1)S(1)}, f32[8,128]{1,0:T(8,128)S(1)}) custom-call(bf16[1,128,1024]{2,1,0:T(8,128)(2,1)} %q_hbm.1, bf16[1,128,1024]{2,1,0:T(8,128)(2,1)} %k_hbm.1, bf16[1,128,1024]{2,1,0:T(8,128)(2,1)} %v_hbm.1, f32[1,8,128]{2,1,0:T(8,128)} %f_hbm.1, ...), custom_call_target="tpu_custom_call" | custom-call | tf_op jit(solution)/shard_map/pallas_call | solution.py:384
  73.4 0.9 %shard_map.94 = (bf16[1,128,1024]{2,1,0:T(8,128)(2,1)}, bf16[1,128,1024]{2,1,0:T(8,128)(2,1)}, bf16[1,128,1024]{2,1,0:T(8,128)(2,1)}, f32[8,128]{1,0:T(8,128)}) custom-call(bf16[1,128,1024]{2,1,0:T(8,128)(2,1)S(1)} %get-tuple-element.12.refs_0_, bf16[1,128,1024]{2,1,0:T(8,128)(2,1)S(1)} %get-tuple-element.13.refs_1_, ...), custom_call_target="tpu_custom_call" | custom-call | tf_op jit(solution)/shard_map/pallas_call | solution.py:409

commit v7 on v6

--- a/solution.py
+++ b/solution.py
@@ -61,16 +61,6 @@
 
     barrier = pltpu.get_barrier_semaphore()
 
-    for i in FAR_FIRST:
-        for peer in (y_peer(i), z_peer(i)):
-            pl.semaphore_signal(barrier, inc=1, device_id=(dp, peer, tn), device_id_type=MESH)
-    for i in range(1, TENSOR):
-        pl.semaphore_signal(
-            barrier, inc=1, device_id=(dp, me, tensor_peer(i)), device_id_type=MESH
-        )
-    pl.semaphore_signal(barrier, inc=1, device_id=(1 - dp, me, tn), device_id_type=MESH)
-    greeted = 2 * (RING - 1) + TENSOR - 1 + 1
-
     loads = [
         pltpu.make_async_copy(source, target, load_sems.at[i])
         for i, (source, target) in enumerate(
@@ -83,6 +73,16 @@
     for load in loads:
         load.start()
 
+    for i in range(1, RING):
+        for peer in (y_peer(i), z_peer(i)):
+            pl.semaphore_signal(barrier, inc=1, device_id=(dp, peer, tn), device_id_type=MESH)
+    for i in range(1, TENSOR):
+        pl.semaphore_signal(
+            barrier, inc=1, device_id=(dp, me, tensor_peer(i)), device_id_type=MESH
+        )
+    pl.semaphore_signal(barrier, inc=1, device_id=(1 - dp, me, tn), device_id_type=MESH)
+    greeted = 2 * (RING - 1) + TENSOR - 1 + 1
+
     def remote(src, dst, send_sem, recv_sem, device):
         return pltpu.make_async_remote_copy(
             src_ref=src, dst_ref=dst, send_sem=send_sem, recv_sem=recv_sem,
@@ -96,7 +96,7 @@
 
     def exchange(src, dst, send_sem, recv_sem, rows):
         for i in FAR_FIRST:
-            peer = lax.rem(y + jnp.where(dp == 0, i, RING - i), RING)
+            peer = lax.rem(y + i, RING)
             remote(
                 src.at[peer, rows], dst.at[y, rows], send_sem, recv_sem,
                 (dp, z * RING + peer, tn),
@@ -104,7 +104,7 @@
         dst[y, rows] = src[y, rows]
 
     def row_peers(later):
-        for i in FAR_FIRST:
+        for i in range(RING - 1, 0, -1):
             peer = z + i if later else z - i
             yield i, peer, (peer < RING) if later else (peer >= 0)
 
@@ -327,6 +327,15 @@
     )
     other_core.start()
     for b in range(BATCHES):
+        wait_bytes(state.at[b, others, FULL], state_send.at[b])
+        row_sent(row_out.at[b], row_send.at[b], True)
+        wait_bytes(prefix.at[b, others], prefix_send.at[b])
+        wait_bytes(back.at[b, others], back_send.at[b])
+        row_sent(row_back_out.at[b], row_back_send.at[b], False)
+    wait_bytes(norm_in.at[pl.ds(0, TENSOR - 1)], norm_sems.at[0])
+    wait_bytes(gain_y_in.at[pl.ds(0, RING - 1)], gain_y_sems.at[0])
+    wait_bytes(gain_z_in.at[pl.ds(0, RING - 1)], gain_z_sems.at[0])
+    for b in range(BATCHES):
         wait_bytes(suffix_in.at[b, others], suffix_recv.at[b])
         for h in range(b * GROUP, (b + 1) * GROUP):
             later_b = get_state(suffix_in, h).astype(BF16)
@@ -339,15 +348,7 @@
     gg_ref[...] = gain_total + gain_dp_in[...]
 
     for b in range(BATCHES):
-        wait_bytes(state.at[b, others, FULL], state_send.at[b])
-        row_sent(row_out.at[b], row_send.at[b], True)
-        wait_bytes(prefix.at[b, others], prefix_send.at[b])
-        wait_bytes(back.at[b, others], back_send.at[b])
-        row_sent(row_back_out.at[b], row_back_send.at[b], False)
         wait_bytes(suffix.at[b, others], suffix_send.at[b])
-    wait_bytes(norm_in.at[pl.ds(0, TENSOR - 1)], norm_sems.at[0])
-    wait_bytes(gain_y_in.at[pl.ds(0, RING - 1)], gain_y_sems.at[0])
-    wait_bytes(gain_z_in.at[pl.ds(0, RING - 1)], gain_z_sems.at[0])
 
 
 def store(*refs):

time: 74.4 us -> 72.4 us (0.973)
  the two profiles are of different devices: /device:TPU:8 before, /device:TPU:64 now
where the time goes in v7:
time: 72.4 us; the launch traced here: 72.3 us
  Pallas kernels  71.6 us (99%)
    pallas_call x1, Pallas kernels, shards(): pl.pallas_call(kernel, out_shape=shapes, in_specs=[hbm] * 6, out_specs=(v...  70.7 us

profile of v7, /device:TPU:64, one launch (start us, length us, event | category | flops | bytes accessed | tf_op | source)
XLA Modules:
  0.0 72.3 jit_solution(18248589050405438098)
XLA Ops:
  0.6 70.7 %shard_map.93 = (bf16[1,128,1024]{2,1,0:T(8,128)(2,1)S(1)}, bf16[1,128,1024]{2,1,0:T(8,128)(2,1)S(1)}, bf16[1,128,1024]{2,1,0:T(8,128)(2,1)S(1)}, f32[8,128]{1,0:T(8,128)S(1)}) custom-call(bf16[1,128,1024]{2,1,0:T(8,128)(2,1)} %q_hbm.1, bf16[1,128,1024]{2,1,0:T(8,128)(2,1)} %k_hbm.1, bf16[1,128,1024]{2,1,0:T(8,128)(2,1)} %v_hbm.1, f32[1,8,128]{2,1,0:T(8,128)} %f_hbm.1, ...), custom_call_target="tpu_custom_call" | custom-call | tf_op jit(solution)/shard_map/pallas_call | solution.py:385
  71.3 0.9 %shard_map.94 = (bf16[1,128,1024]{2,1,0:T(8,128)(2,1)}, bf16[1,128,1024]{2,1,0:T(8,128)(2,1)}, bf16[1,128,1024]{2,1,0:T(8,128)(2,1)}, f32[8,128]{1,0:T(8,128)}) custom-call(bf16[1,128,1024]{2,1,0:T(8,128)(2,1)S(1)} %get-tuple-element.12.refs_0_, bf16[1,128,1024]{2,1,0:T(8,128)(2,1)S(1)} %get-tuple-element.13.refs_1_, ...), custom_call_target="tpu_custom_call" | custom-call | tf_op jit(solution)/shard_map/pallas_call | solution.py:410
